TPU v7x, 32 devices: a whole 2x2x4 slice. The times are simulated.
32 devices in a mesh: expert: 32 (over z, y, x, core), dp: 1.
Axes of the slice: x: 2, y: 2, z: 4, core: 2. Of those that a mesh axis runs over, the one named last changes fastest.
Arguments:
- tokens: bfloat16 [512, 7168], P(('dp', 'expert')), may hold values from -6 to 6
- slot_ids: int32 [512, 4], P(('dp', 'expert')), may hold values from 0 to 7, all different within a row; in each aligned block of 16 rows (0 to 15, 16 to 31, ...) at most 16 rows name the same one
- route_weights: float32 [512, 4], P(('dp', 'expert')), may hold values from 0.2 to 1
- pair_swap: int32 [4], replicated, may hold values from 0 to 1, as said below
- w_gate: bfloat16 [32, 7168, 256], P('expert'), may hold values from -0.0625 to 0.0625
- w_up: bfloat16 [32, 7168, 256], P('expert'), may hold values from -0.0625 to 0.0625
- w_down: bfloat16 [32, 256, 7168], P('expert'), may hold values from -0.1875 to 0.1875
Outputs:
- mixed: bfloat16 [512, 7168], P(('dp', 'expert'))
Inputs may be any that keep to these rules, and one draw needn't show every extreme that they name: `slot_ids`: each row names 4 different slots; among the rows of one device no slot is named more than 16 times, a bound that some block reaches. `pair_swap`: some pair trades its weights and some pair does not.
All inputs are finite; a program needn't handle non-finite values.
Results may differ from a plain program's by a relative error of at most 0.0059.
Values may be sent and summed in bfloat16 or wider, within the bound.
A program may use at most 128 MiB of HBM per device.

v0:
```python
import jax
import jax.numpy as jnp
from jax import lax
from jax.sharding import PartitionSpec as P


def from_partner(block, axis, apart):
    count = lax.axis_size(axis)
    route = []
    for low in range(count):
        high = low | 1 << apart
        if high != low and high < count:
            route += [(low, high), (high, low)]
    return lax.ppermute(block, axis, route)


def on_device(tokens, slot_ids, route_weights, pair_swap, w_gate, w_up, w_down):
    blocks = lax.axis_size("expert")
    pairs = pair_swap.shape[0]
    slots = 2 * pairs
    span = blocks // slots
    rows, width = tokens.shape
    top = slot_ids.shape[1]
    capacity = min(rows, 2 * rows * top // slots)
    own_slot = lax.axis_index("expert") % slots
    pair_iota = jnp.arange(pairs, dtype=jnp.int32)
    moved = jnp.sum(jnp.where(pair_iota == own_slot // 2, pair_swap, 0)) > 0
    partner = from_partner((w_gate, w_up, w_down), "expert", 0)
    gate_block = jnp.where(moved, partner[0], w_gate)[0]
    up_block = jnp.where(moved, partner[1], w_up)[0]
    down_block = jnp.where(moved, partner[2], w_down)[0]
    picks = slot_ids.reshape(-1)
    one_hot = (picks[:, None] == jnp.arange(slots, dtype=jnp.int32)).astype(jnp.int32)
    before = jnp.cumsum(one_hot, 0) - one_hot
    position = jnp.sum(before * one_hot, 1)
    entry = picks * capacity + position
    table = (entry[:, None] == jnp.arange(slots * capacity, dtype=jnp.int32)).astype(jnp.float32)
    table = table.reshape(rows, top, slots * capacity)
    row_mask = jnp.sum(table, 1).astype(jnp.bfloat16)
    weighted = jnp.sum(table * route_weights[:, :, None], 1)
    packed = jnp.dot(row_mask.T, tokens, preferred_element_type=jnp.float32).astype(jnp.bfloat16)
    packed = packed.reshape(slots, capacity, width)
    outgoing = jnp.tile(packed, (span, 1, 1))
    received = lax.all_to_all(outgoing, "expert", split_axis=0, concat_axis=0, tiled=True)
    count = received.shape[1]
    flat = received.reshape(-1, width)
    gate = jnp.dot(flat, gate_block, preferred_element_type=jnp.float32)
    up = jnp.dot(flat, up_block, preferred_element_type=jnp.float32)
    hidden = (jax.nn.silu(gate) * up).astype(jnp.bfloat16)
    partial_value = jnp.dot(hidden, down_block, preferred_element_type=jnp.float32).astype(
        jnp.bfloat16
    )
    partial_value = partial_value.reshape(blocks, count, width)
    returned = lax.all_to_all(partial_value, "expert", split_axis=0, concat_axis=0, tiled=True)
    summed = jnp.sum(returned.reshape(span, slots, capacity, width).astype(jnp.float32), 0)
    summed = summed.reshape(slots * capacity, width)
    mixed = jnp.dot(
        weighted, summed, precision=lax.Precision.HIGHEST, preferred_element_type=jnp.float32
    )
    return mixed.astype(jnp.bfloat16)


def solution(mesh):
    return jax.shard_map(
        on_device,
        mesh=mesh,
        in_specs=(
            P(("dp", "expert"), None),
            P(("dp", "expert"), None),
            P(("dp", "expert"), None),
            P(),
            P("expert", None, None),
            P("expert", None, None),
            P("expert", None, None),
        ),
        out_specs=P(("dp", "expert"), None),
        check_vma=False,
    )
```

profile of v0, /device:TPU:1, one launch (start us, length us, event | category | flops | bytes accessed | tf_op | source)
XLA Modules:
  0.0 360.7 jit_solution(10661441065231890412)
XLA Ops:
  0.0 0.0 copy-start
  0.0 0.8 copy.17
  0.8 0.1 eq.37
  0.9 0.1 fusion.12
  1.0 0.1 reduce_window_sum.11
  1.1 0.2 select_reduce_fusion.1
  1.2 0.1 reduce_sum.48
  1.3 0.1 copy.18
  1.4 0.7 multiply_add_fusion
  2.1 0.8 convert_reduce_fusion.1
  2.9 0.0 copy-done
  2.9 0.7 convolution_convert_fusion.1
  3.6 3.9 %tile.11 = bf16[4,8,16,7168]{3,2,1,0:T(8,128)(2,1)} broadcast(bf16[8,16,7168]{2,1,0:T(8,128)(2,1)S(1)} %bitcast.26), dimensions={1,2,3} | broadcast | bytes 9175040 | tf_op jit(solution)/shard_map/tile | solution.py:43
  7.5 0.0 copy-start.3
  7.5 7.1 %all-to-all-start = ((bf16[32,16,7168]{2,1,0:T(8,128)(2,1)}), bf16[32,16,7168]{2,1,0:T(8,128)(2,1)}, u32[]{:S(2)}, u32[]{:S(2)}) async-start(bf16[32,16,7168]{2,1,0:T(8,128)(2,1)} %bitcast.23), calls=%async_computation | async-start | bytes 14680064 | tf_op jit(solution)/shard_map/all_to_all | solution.py:44
  14.6 0.4 collective-permute-start.1
  15.0 0.2 collective-permute-start
  15.2 0.3 collective-permute-start.2
  15.5 0.0 copy-done.3
  15.5 0.6 fusion.14
  16.8 4.6 %collective-permute-done.1 = bf16[1,7168,256]{2,1,0:T(8,128)(2,1)} collective-permute-done((bf16[1,7168,256]{2,1,0:T(8,128)(2,1)}, bf16[1,7168,256]{2,1,0:T(8,128)(2,1)}, u32[]{:S(2)}, u32[]{:S(2)}) %collective-permute-start.1) | collective-permute-done | bytes 3670048 | tf_op jit(solution)/shard_map/ppermute | solution.py:14
  21.4 155.7 %all-to-all-done = bf16[32,16,7168]{2,1,0:T(8,128)(2,1)} async-done(((bf16[32,16,7168]{2,1,0:T(8,128)(2,1)}), bf16[32,16,7168]{2,1,0:T(8,128)(2,1)}, u32[]{:S(2)}, u32[]{:S(2)}) %all-to-all-start) | async-done | bytes 7340064 | tf_op jit(solution)/shard_map/all_to_all | solution.py:44
  177.2 0.0 copy-start.2
  177.2 6.3 %fusion.1 = f32[512,256]{1,0:T(8,128)S(1)} fusion(bf16[512,7168]{1,0:T(8,128)(2,1)} %bitcast.2, bf16[1,7168,256]{2,1,0:T(8,128)(2,1)} %collective-permute-done.1, bf16[1,7168,256]{2,1,0:T(8,128)(2,1)} %param.12, pred[]{:T(512)S(6)} %gt.3), kind=kOutput, calls=%fused_computation.5 | convolution fusion | flops 1880883200 | bytes 15204353 | tf_op jit(solution)/shard_map/dot_general | solution.py:48
  183.5 0.0 copy-start.1
  183.5 0.0 collective-permute-done
  183.5 0.0 copy-done.2
  183.6 6.4 %fusion.3 = f32[512,256]{1,0:T(8,128)S(1)} fusion(bf16[512,7168]{1,0:T(8,128)(2,1)} %bitcast.2, bf16[1,7168,256]{2,1,0:T(8,128)(2,1)} %collective-permute-done, bf16[1,7168,256]{2,1,0:T(8,128)(2,1)S(1)} %copy-done.2, pred[]{:T(512)S(6)} %gt.3), kind=kOutput, calls=%fused_computation.7 | convolution fusion | flops 1880883200 | bytes 15204353 | tf_op jit(solution)/shard_map/dot_general | solution.py:47
  190.0 0.0 collective-permute-done.2
  190.0 0.0 copy-done.1
  190.0 4.2 %convolution_convert_fusion = bf16[512,7168]{1,0:T(8,128)(2,1)S(1)} fusion(bf16[1,256,7168]{2,1,0:T(8,128)(2,1)} %collective-permute-done.2, bf16[1,256,7168]{2,1,0:T(8,128)(2,1)S(1)} %copy-done.1, pred[]{:T(512)S(6)} %gt.3, f32[512,256]{1,0:T(8,128)S(1)} %fusion.1, f32[512,256]{1,0:T(8,128)S(1)} %fusion.3), kind=kOutput, calls=%fused_computation.1 | convolution fusion | flops 1885339648 | bytes 15728641 | tf_op jit(solution)/shard_map/dot_general | solution.py:50
  194.2 162.6 %all_to_all.10 = bf16[32,16,7168]{2,1,0:T(8,128)(2,1)S(1)} all-to-all(bf16[32,16,7168]{2,1,0:T(8,128)(2,1)S(1)} %bitcast.22), channel_id=1, replica_groups=mesh['expert'=32,'dp'=1] {'expert'}, dimensions={0} | all-to-all | bytes 14680064 | tf_op jit(solution)/shard_map/all_to_all | solution.py:54
  356.8 1.3 convert_reduce_fusion
  358.2 2.5 convolution_convert_fusion.2
Async XLA Ops:
  0.0 2.9 copy-start
  7.5 8.1 %copy-start.3 = (s32[4]{0:T(128)S(1)}, s32[4]{0:T(128)}, u32[]{:S(2)}) copy-start(s32[4]{0:T(128)} %param.10) | copy-start | bytes 52
  7.5 169.7 %all-to-all-start = ((bf16[32,16,7168]{2,1,0:T(8,128)(2,1)}), bf16[32,16,7168]{2,1,0:T(8,128)(2,1)}, u32[]{:S(2)}, u32[]{:S(2)}) async-start(bf16[32,16,7168]{2,1,0:T(8,128)(2,1)} %bitcast.23), calls=%async_computation | async-start | bytes 14680064 | tf_op jit(solution)/shard_map/all_to_all | solution.py:44
  14.6 6.8 %collective-permute-start.1 = (bf16[1,7168,256]{2,1,0:T(8,128)(2,1)}, bf16[1,7168,256]{2,1,0:T(8,128)(2,1)}, u32[]{:S(2)}, u32[]{:S(2)}) collective-permute-start(bf16[1,7168,256]{2,1,0:T(8,128)(2,1)} %param.12), channel_id=1, source_target_pairs={{0,1},{1,0},{2,3},{3,2},{4,5},{5,4},{6,7},{7,6},{8,9},{9,8},{10,11... | collective-permute-start | bytes 11010056 | tf_op jit(solution)/shard_map/ppermute | solution.py:14
  15.0 168.5 %collective-permute-start = (bf16[1,7168,256]{2,1,0:T(8,128)(2,1)}, bf16[1,7168,256]{2,1,0:T(8,128)(2,1)}, u32[]{:S(2)}, u32[]{:S(2)}) collective-permute-start(bf16[1,7168,256]{2,1,0:T(8,128)(2,1)} %param.11), channel_id=1, source_target_pairs={{0,1},{1,0},{2,3},{3,2},{4,5},{5,4},{6,7},{7,6},{8,9},{9,8},{10,11... | collective-permute-start | bytes 11010056 | tf_op jit(solution)/shard_map/ppermute | solution.py:14
  15.2 174.8 %collective-permute-start.2 = (bf16[1,256,7168]{2,1,0:T(8,128)(2,1)}, bf16[1,256,7168]{2,1,0:T(8,128)(2,1)}, u32[]{:S(2)}, u32[]{:S(2)}) collective-permute-start(bf16[1,256,7168]{2,1,0:T(8,128)(2,1)} %param.13), channel_id=1, source_target_pairs={{0,1},{1,0},{2,3},{3,2},{4,5},{5,4},{6,7},{7,6},{8,9},{9,8},{10,11... | collective-permute-start | bytes 11010056 | tf_op jit(solution)/shard_map/ppermute | solution.py:14
  177.2 6.4 %copy-start.2 = (bf16[1,7168,256]{2,1,0:T(8,128)(2,1)S(1)}, bf16[1,7168,256]{2,1,0:T(8,128)(2,1)}, u32[]{:S(2)}) copy-start(bf16[1,7168,256]{2,1,0:T(8,128)(2,1)} %param.11) | copy-start | bytes 11010052
  183.5 6.5 %copy-start.1 = (bf16[1,256,7168]{2,1,0:T(8,128)(2,1)S(1)}, bf16[1,256,7168]{2,1,0:T(8,128)(2,1)}, u32[]{:S(2)}) copy-start(bf16[1,256,7168]{2,1,0:T(8,128)(2,1)} %param.13) | copy-start | bytes 11010052
where the time goes:
time: 361 us
  blocking collectives  163 us (45%)
  waiting for transfers between devices  160 us (44%)
  matrix products  20.2 us (6%)
  starting transfers between devices  8.05 us (2%)
  local copies, waits for them, and re-layouts  4.98 us (1%)
  other arithmetic  3.78 us (1%)
    all_to_all x1, blocking collectives, on_device(): lax.all_to_all(partial_value, 'expert', split_axis=0, concat_axis=0, tile...  163 us
    all_to_all x1, waiting for transfers between devices, on_device(): lax.all_to_all(outgoing, 'expert', split_axis=0, concat_axis=0, tiled=True)  156 us
  transfers between devices with their start and end apart: 4, of which 2 were waited for; matrix products, arithmetic and copies ran while one was open for 4% of the time, Pallas kernels for 0%

commit v1 on v0

v1 whole, which is shorter than its diff:
```python
import functools
import jax
import jax.numpy as jnp
from jax import lax
from jax.experimental import pallas as pl
from jax.experimental.pallas import tpu as pltpu
from jax.sharding import PartitionSpec as P

LANES = 128
CORE, ALONG_X, ALONG_Y = 1, 2, 4
SQUARE_SLOTS = 8


def flipped(index, bit):
    return index + bit - 2 * bit * ((index // bit) % 2)


def kernel(
    span,
    pair_ref,
    ids_ref,
    route_ref,
    tokens_hbm,
    gate_hbm,
    up_hbm,
    down_hbm,
    out_ref,
    tok,
    wg,
    wu,
    wd,
    gate_acc,
    up_acc,
    hid,
    hid_out,
    own_sum,
    x_pend,
    y_pend,
    x_out,
    y_out,
    d_out,
    x_in,
    y_in,
    d_in,
    z_out,
    z_in,
    local_sem,
    send_sem,
    recv_sem,
):
    rows, width = out_ref.shape
    slots = SQUARE_SLOTS
    half = width // 2
    me = lax.axis_index("expert")
    own = me % slots
    z = me // slots
    c = me % 2
    x_peer, y_peer, core_peer = flipped(me, ALONG_X), flipped(me, ALONG_Y), flipped(me, CORE)

    def along_z(k, base):
        return ((z + k) % span) * slots + base

    partners = [along_z(k, own) for k in range(1, span)]
    partners += [along_z(k, flipped(own, CORE)) for k in range(span)]
    partners += [x_peer, y_peer]

    my_half = pl.ds(pl.multiple_of(c * half, LANES), half)
    other_half = pl.ds(pl.multiple_of((1 - c) * half, LANES), half)

    loads = [
        pltpu.make_async_copy(tokens_hbm, tok.at[0, 0, 0, :, pl.ds(0, width)], local_sem.at[0]),
        pltpu.make_async_copy(gate_hbm.at[0], wg, local_sem.at[1]),
        pltpu.make_async_copy(up_hbm.at[0], wu, local_sem.at[2]),
        pltpu.make_async_copy(down_hbm.at[0, :, my_half], wd.at[0], local_sem.at[3]),
    ]
    for load in loads:
        load.start()

    barrier = pltpu.get_barrier_semaphore()
    for partner in partners:
        pl.semaphore_signal(
            barrier, inc=1, device_id={"expert": partner}, device_id_type=pl.DeviceIdType.MESH
        )

    lane = lax.broadcasted_iota(jnp.int32, (rows, LANES), 1)
    dense = jnp.zeros((rows, LANES), jnp.float32)
    for k in range(ids_ref.shape[1]):
        dense += jnp.where(ids_ref[:, k : k + 1] == lane % slots, route_ref[:, k : k + 1], 0.0)
    first = dense.astype(jnp.bfloat16).astype(jnp.float32)
    second = (dense - first).astype(jnp.bfloat16).astype(jnp.float32)
    third = dense - first - second
    term = lane // slots
    coded = jnp.where(
        term == 0, first, jnp.where(term == 1, second, jnp.where(term == 2, third, 0.0))
    )
    tok[0, 0, 0, :, pl.ds(width, LANES)] = coded.astype(jnp.bfloat16)

    swap = pair_ref[own // 2]
    slot = own + swap * (1 - 2 * (own % 2))

    count = [0]
    sent = []

    def message(src, dst, device):
        i = count[0]
        count[0] += 1
        return pltpu.make_async_remote_copy(
            src_ref=src,
            dst_ref=dst,
            send_sem=send_sem.at[i],
            recv_sem=recv_sem.at[i],
            device_id={"expert": device},
            device_id_type=pl.DeviceIdType.MESH,
        )

    def start(copy):
        copy.start()
        sent.append(copy)

    left, right = pl.ds(0, half), pl.ds(half, half + LANES)
    by_z = {
        p: message(tok.at[0, 0, 0], tok.at[0, 0, p], along_z(span - p, own)) for p in range(1, span)
    }
    by_x = [message(tok.at[0, 0, p], tok.at[1, 0, p], x_peer) for p in range(span)]
    by_y = [message(tok.at[0, 0, p], tok.at[2, 0, p], y_peer) for p in range(span)]
    to_core = [
        [message(tok.at[g, 0, p], tok.at[g, 1, p], core_peer) for p in range(span)] for g in range(3)
    ]
    far_left = [
        message(tok.at[1, 0, p, :, left], tok.at[3, 0, p, :, left], y_peer) for p in range(span)
    ]
    far_right = [
        message(tok.at[2, 0, p, :, right], tok.at[3, 0, p, :, right], x_peer) for p in range(span)
    ]
    core_left = [
        message(tok.at[3, 0, p, :, left], tok.at[3, 1, p, :, left], core_peer) for p in range(span)
    ]
    core_right = [
        message(tok.at[3, 0, p, :, right], tok.at[3, 1, p, :, right], core_peer)
        for p in range(span)
    ]
    swap_down = message(down_hbm.at[0, :, other_half], wd.at[1], core_peer)
    swap_hidden = [message(hid_out.at[g], hid.at[g, 1], core_peer) for g in range(4)]
    x_early = message(x_out.at[0], x_in.at[0], x_peer)
    y_early = message(y_out.at[1], y_in.at[1], y_peer)
    d_to_x = [message(d_out.at[0, p], d_in.at[0, p], x_peer) for p in range(span)]
    d_to_y = [message(d_out.at[1, p], d_in.at[1, p], y_peer) for p in range(span)]
    x_late = [message(x_out.at[1, p], x_in.at[1, p], x_peer) for p in range(span)]
    y_late = [message(y_out.at[0, p], y_in.at[0, p], y_peer) for p in range(span)]
    home = {
        (r, p): message(
            z_out.at[r, p],
            z_in.at[r, (span - p) % span],
            along_z(p, own if r == 0 else flipped(own, CORE)),
        )
        for r in range(2)
        for p in range(span)
        if (r, p) != (0, 0)
    }

    def project(g):
        depth = 1024 if width % 1024 == 0 else width
        gate_acc[...] = jnp.zeros_like(gate_acc)
        up_acc[...] = jnp.zeros_like(up_acc)

        def step(i, _):
            part = pl.ds(pl.multiple_of(i * depth, LANES), depth)
            x = tok[g, :, :, :, part].reshape(2 * span * rows, depth)
            gate_acc[...] += jnp.dot(x, wg[part, :], preferred_element_type=jnp.float32)
            up_acc[...] += jnp.dot(x, wu[part, :], preferred_element_type=jnp.float32)
            return 0

        lax.fori_loop(0, width // depth, step, 0)
        code = tok[g, :, :, :, pl.ds(width, LANES)].reshape(2 * span * rows, LANES)
        lanes = lax.broadcasted_iota(jnp.int32, code.shape, 1)
        weight = jnp.sum(
            jnp.where(lanes % slots == slot, code.astype(jnp.float32), 0.0), 1, keepdims=True
        )
        gate = gate_acc[...]
        value = (gate / (1.0 + jnp.exp(-gate)) * up_acc[...] * weight).astype(jnp.bfloat16)
        many = span * rows
        hid[g, 0] = value
        hid_out[g, pl.ds(0, many)] = value[many:]
        hid_out[g, pl.ds(many, many)] = value[:many]
        start(swap_hidden[g])

    def expand(g, first_to, second_to):
        wide = 512 if half % 512 == 0 else half
        many = span * rows
        swap_hidden[g].wait_recv()

        def step(i, _):
            part = pl.ds(pl.multiple_of(i * wide, LANES), wide)
            total = jnp.dot(hid[g, 0], wd[0, :, part], preferred_element_type=jnp.float32)
            total += jnp.dot(hid[g, 1], wd[1, :, part], preferred_element_type=jnp.float32)
            for ref, piece in ((first_to, total[:many]), (second_to, total[many:])):
                ref[:, :, part] = piece.reshape(span, rows, wide).astype(ref.dtype)
            return 0

        lax.fori_loop(0, half // wide, step, 0)

    def gathered(p):
        if p:
            by_z[p].wait_recv()
        start(by_x[p])
        start(by_y[p])
        start(to_core[0][p])

    def crossed(p):
        by_x[p].wait_recv()
        start(far_left[p])
        start(to_core[1][p])
        by_y[p].wait_recv()
        start(far_right[p])
        start(to_core[2][p])

    def cornered(p):
        far_left[p].wait_recv()
        start(core_left[p])
        far_right[p].wait_recv()
        start(core_right[p])

    loads[0].wait()
    pl.semaphore_wait(barrier, len(partners))
    for p in range(1, span):
        start(by_z[p])
    gathered(0)
    start(swap_down)
    order = [p for p in (1, span - 1) if p < span] + list(range(2, span - 1))
    done = [0]
    for p in order:
        gathered(p)
        crossed(done[-1])
        if len(done) > 1:
            cornered(done[-2])
        done.append(p)
    for load in loads[1:3]:
        load.wait()
    for p in range(span):
        to_core[0][p].wait_recv()
    project(0)
    crossed(done[-1])
    cornered(done[-2])
    for p in range(span):
        to_core[1][p].wait_recv()
    project(1)
    cornered(done[-1])
    for p in range(span):
        to_core[2][p].wait_recv()
    project(2)
    loads[3].wait()
    swap_down.wait_recv()
    expand(1, x_out.at[0], x_pend)
    start(x_early)
    expand(2, y_pend, y_out.at[1])
    start(y_early)
    for p in range(span):
        core_left[p].wait_recv()
        core_right[p].wait_recv()
    project(3)
    expand(0, own_sum.at[0], own_sum.at[1])
    expand(3, d_out.at[0], d_out.at[1])
    order = order + [0]
    for p in order:
        start(d_to_x[p])
        start(d_to_y[p])
    for p in order:
        d_to_y[p].wait_recv()
        x_out[1, p] = (x_pend[p] + d_in[1, p].astype(jnp.float32)).astype(jnp.bfloat16)
        start(x_late[p])
        d_to_x[p].wait_recv()
        y_out[0, p] = (y_pend[p] + d_in[0, p].astype(jnp.float32)).astype(jnp.bfloat16)
        start(y_late[p])
    x_early.wait_recv()
    y_early.wait_recv()
    for p in order:
        x_late[p].wait_recv()
        y_late[p].wait_recv()
        for r in range(2):
            total = own_sum[r, p] + x_in[r, p].astype(jnp.float32) + y_in[r, p].astype(jnp.float32)
            if (r, p) == (0, 0):
                own_sum[r, p] = total
            else:
                z_out[r, p] = total.astype(jnp.bfloat16)
                start(home[r, p])
    for copy in home.values():
        copy.wait_recv()
    total = own_sum[0, 0]
    for p in range(1, span):
        total += z_in[0, p].astype(jnp.float32)
    out_ref[:, my_half] = total.astype(jnp.bfloat16)
    total = z_in[1, 0].astype(jnp.float32)
    for p in range(1, span):
        total += z_in[1, p].astype(jnp.float32)
    out_ref[:, other_half] = total.astype(jnp.bfloat16)
    for copy in sent:
        copy.wait_send()


def squares(tokens, slot_ids, route_weights, pair_swap, w_gate, w_up, w_down):
    span = lax.axis_size("expert") // SQUARE_SLOTS
    rows, width = tokens.shape
    hidden = w_gate.shape[2]
    half = width // 2
    wide = width + LANES
    group = 2 * span * rows
    messages = (span - 1) + 9 * span + 1 + 4 + 2 + 4 * span + 2 * span - 1
    bf16, f32 = jnp.bfloat16, jnp.float32
    column = (span, rows, half)
    vmem = pl.BlockSpec(memory_space=pltpu.VMEM)
    hbm = pl.BlockSpec(memory_space=pl.ANY)
    return pl.pallas_call(
        functools.partial(kernel, span),
        out_shape=jax.ShapeDtypeStruct((rows, width), bf16),
        in_specs=[pl.BlockSpec(memory_space=pltpu.SMEM), vmem, vmem, hbm, hbm, hbm, hbm],
        out_specs=vmem,
        scratch_shapes=[
            pltpu.VMEM((4, 2, span, rows, wide), bf16),
            pltpu.VMEM((width, hidden), bf16),
            pltpu.VMEM((width, hidden), bf16),
            pltpu.VMEM((2, hidden, half), bf16),
            pltpu.VMEM((group, hidden), f32),
            pltpu.VMEM((group, hidden), f32),
            pltpu.VMEM((4, 2, group, hidden), bf16),
            pltpu.VMEM((4, group, hidden), bf16),
            pltpu.VMEM((2,) + column, f32),
            pltpu.VMEM(column, f32),
            pltpu.VMEM(column, f32),
        ]
        + [pltpu.VMEM((2,) + column, bf16)] * 8
        + [
            pltpu.SemaphoreType.DMA((4,)),
            pltpu.SemaphoreType.DMA((messages,)),
            pltpu.SemaphoreType.DMA((messages,)),
        ],
        compiler_params=pltpu.CompilerParams(
            collective_id=0, has_side_effects=True, vmem_limit_bytes=56 * 2**20
        ),
    )(pair_swap, slot_ids, route_weights, tokens, w_gate, w_up, w_down)


def whole(tokens, slot_ids, route_weights, pair_swap, w_gate, w_up, w_down):
    slots = 2 * pair_swap.shape[0]
    own = lax.axis_index("expert") % slots
    pair = jnp.arange(pair_swap.shape[0], dtype=jnp.int32)
    swap = jnp.sum(jnp.where(pair == own // 2, pair_swap, 0))
    slot = own + swap * (1 - 2 * (own % 2))
    named = slot_ids[:, :, None] == jnp.arange(slots, dtype=jnp.int32)
    dense = jnp.sum(jnp.where(named, route_weights[:, :, None], 0.0), 1)
    rows = lax.all_gather(tokens, "expert", axis=0, tiled=True)
    dense = lax.all_gather(dense, "expert", axis=0, tiled=True)
    mine = jnp.arange(slots, dtype=jnp.int32) == slot
    weight = jnp.sum(jnp.where(mine, dense, 0.0), 1, keepdims=True)
    gate = jnp.dot(rows, w_gate[0], preferred_element_type=jnp.float32)
    up = jnp.dot(rows, w_up[0], preferred_element_type=jnp.float32)
    hidden = (jax.nn.silu(gate) * up).astype(jnp.bfloat16)
    value = jnp.dot(hidden, w_down[0], preferred_element_type=jnp.float32) * weight
    mixed = lax.psum_scatter(value, "expert", scatter_dimension=0, tiled=True)
    return mixed.astype(jnp.bfloat16)


def on_device(*args):
    slots = 2 * args[3].shape[0]
    return (squares if slots == SQUARE_SLOTS else whole)(*args)


def solution(mesh):
    return jax.shard_map(
        on_device,
        mesh=mesh,
        in_specs=(
            P(("dp", "expert"), None),
            P(("dp", "expert"), None),
            P(("dp", "expert"), None),
            P(),
            P("expert", None, None),
            P("expert", None, None),
            P("expert", None, None),
        ),
        out_specs=P(("dp", "expert"), None),
        check_vma=False,
    )
```

time: 361 us -> 102 us (0.28)
  blocking collectives: 163 us -> 0 us
  waiting for transfers between devices: 160 us -> 0 us
  Pallas kernels: 0 us -> 97.2 us
  matrix products: 20.2 us -> 0 us
  starting transfers between devices: 8.05 us -> 0 us
  other arithmetic: 3.78 us -> 0 us
    all_to_all x1 -> x0, blocking collectives: 163 us -> none  [on_device(): lax.all_to_all(partial_value, 'expert', split_axis=0, concat_axis=0, tile...]
    all_to_all x1 -> x0, waiting for transfers between devices: 156 us -> none  [on_device(): lax.all_to_all(outgoing, 'expert', split_axis=0, concat_axis=0, tiled=True)]
    pallas_call x0 -> x1, Pallas kernels: none -> 97.2 us  [squares(): pl.pallas_call(functools.partial(kernel, span), out_shape=jax.ShapeDtypeS...]
    dot_general x5 -> x0, matrix products: 20.2 us -> none  [the longest x1 6.44 us: on_device(): gate = jnp.dot(flat, gate_block, preferred_element_type=jnp.float32)]
    all_to_all x1 -> x0, starting transfers between devices: 7.15 us -> none  [on_device(): lax.all_to_all(outgoing, 'expert', split_axis=0, concat_axis=0, tiled=True)]
    ppermute x3 -> x0, waiting for transfers between devices: 4.63 us -> none  [from_partner(): return lax.ppermute(block, axis, route)]
    another operation x1 -> x0, local copies, waits for them, and re-layouts: 3.91 us -> none  [on_device(): outgoing = jnp.tile(packed, (span, 1, 1))]
  transfers between devices with their start and end apart: 4 -> 0, of which waited for: 2 -> 0; matrix products, arithmetic and copies ran while one was open for 4% -> 0% of each run, Pallas kernels for 0% -> 0%
where the time goes in v1:
time: 102 us
  Pallas kernels  97.2 us (95%)
  local copies, waits for them, and re-layouts  4.35 us (4%)
    pallas_call x1, Pallas kernels, squares(): pl.pallas_call(functools.partial(kernel, span), out_shape=jax.ShapeDtypeS...  97.2 us
    unnamed x3, local copies, waits for them, and re-layouts  4.35 us

profile of v1, /device:TPU:1, one launch (start us, length us, event | category | flops | bytes accessed | tf_op | source)
XLA Modules:
  0.0 101.6 jit_solution(16405506047005491713)
XLA Ops:
  0.0 1.4 %copy.8.ids_ref = s32[16,4]{1,0:T(8,128)} copy(s32[16,4]{0,1:T(4,128)} %param.8) | data formatting | bytes 512 | tf_op args[1]
  1.4 1.4 %copy.9.route_ref = f32[16,4]{1,0:T(8,128)} copy(f32[16,4]{0,1:T(4,128)} %param.9) | data formatting | bytes 512 | tf_op args[2]
  2.7 97.2 %shard_map.73 = bf16[16,7168]{1,0:T(8,128)(2,1)} custom-call(s32[4]{0:T(128)} %pair_ref.1, s32[16,4]{1,0:T(8,128)} %copy.8.ids_ref, f32[16,4]{1,0:T(8,128)} %copy.9.route_ref, bf16[16,7168]{1,0:T(8,128)(2,1)} %tokens_hbm.1, bf16[1,7168,256]{2,1,0:T(8,128)(2,1)} %gate_hbm.1, bf16[1,7168,256]{2,1,0:T(8,128)(2,1)} %up_hbm.1, bf16[1,256,7168]{2,1,0:T(8,128)(2,1)} %down_hbm.1), custom_call_target="tpu_custom_call" | custom-call | tf_op jit(solution)/shard_map/pallas_call | solution.py:312
  99.9 1.6 %copy.11 = bf16[16,7168]{1,0:T(8,128)(2,1)} copy(bf16[16,7168]{1,0:T(8,128)(2,1)} %shard_map.73) | data formatting | bytes 458752

commit v2 on v1

--- a/solution.py
+++ b/solution.py
@@ -9,6 +9,7 @@
 LANES = 128
 CORE, ALONG_X, ALONG_Y = 1, 2, 4
 SQUARE_SLOTS = 8
+COLUMN = 4
 
 
 def flipped(index, bit):
@@ -47,6 +48,8 @@
     local_sem,
     send_sem,
     recv_sem,
+    chain_send,
+    chain_recv,
 ):
     rows, width = out_ref.shape
     slots = SQUARE_SLOTS
@@ -68,7 +71,7 @@
     other_half = pl.ds(pl.multiple_of((1 - c) * half, LANES), half)
 
     loads = [
-        pltpu.make_async_copy(tokens_hbm, tok.at[0, 0, 0, :, pl.ds(0, width)], local_sem.at[0]),
+        pltpu.make_async_copy(tokens_hbm, tok.at[0, 0, z, :, pl.ds(0, width)], local_sem.at[0]),
         pltpu.make_async_copy(gate_hbm.at[0], wg, local_sem.at[1]),
         pltpu.make_async_copy(up_hbm.at[0], wu, local_sem.at[2]),
         pltpu.make_async_copy(down_hbm.at[0, :, my_half], wd.at[0], local_sem.at[3]),
@@ -82,18 +85,27 @@
             barrier, inc=1, device_id={"expert": partner}, device_id_type=pl.DeviceIdType.MESH
         )
 
-    lane = lax.broadcasted_iota(jnp.int32, (rows, LANES), 1)
-    dense = jnp.zeros((rows, LANES), jnp.float32)
-    for k in range(ids_ref.shape[1]):
-        dense += jnp.where(ids_ref[:, k : k + 1] == lane % slots, route_ref[:, k : k + 1], 0.0)
+    line = lax.broadcasted_iota(jnp.int32, (LANES, rows), 0)
+    dense = jnp.zeros((LANES, rows), jnp.float32)
+    for k in range(ids_ref.shape[0]):
+        dense += jnp.where(ids_ref[k : k + 1, :] == line % slots, route_ref[k : k + 1, :], 0.0)
     first = dense.astype(jnp.bfloat16).astype(jnp.float32)
     second = (dense - first).astype(jnp.bfloat16).astype(jnp.float32)
     third = dense - first - second
-    term = lane // slots
+    term = line // slots
     coded = jnp.where(
         term == 0, first, jnp.where(term == 1, second, jnp.where(term == 2, third, 0.0))
     )
-    tok[0, 0, 0, :, pl.ds(width, LANES)] = coded.astype(jnp.bfloat16)
+    same = lax.broadcasted_iota(jnp.int32, (rows, rows), 0) == lax.broadcasted_iota(
+        jnp.int32, (rows, rows), 1
+    )
+    turned = lax.dot_general(
+        jnp.where(same, 1.0, 0.0).astype(jnp.bfloat16),
+        coded.astype(jnp.bfloat16),
+        (((1,), (1,)), ((), ())),
+        preferred_element_type=jnp.float32,
+    )
+    tok[0, 0, z, :, pl.ds(width, LANES)] = turned.astype(jnp.bfloat16)
 
     swap = pair_ref[own // 2]
     slot = own + swap * (1 - 2 * (own % 2))
@@ -101,58 +113,78 @@
     count = [0]
     sent = []
 
-    def message(src, dst, device):
-        i = count[0]
-        count[0] += 1
+    def family(size, route):
+        base = count[0]
+        count[0] += size
+
+        def member(i, number=None):
+            at = base + (i if number is None else number)
+            src, dst, device = route(i)
+            return pltpu.make_async_remote_copy(
+                src_ref=src,
+                dst_ref=dst,
+                send_sem=send_sem.at[at],
+                recv_sem=recv_sem.at[at],
+                device_id={"expert": device},
+                device_id_type=pl.DeviceIdType.MESH,
+            )
+
+        return member
+
+    def start(copy):
+        copy.start()
+        sent.append(copy)
+
+    left, right = pl.ds(0, half), pl.ds(half, half + LANES)
+    upper = jnp.minimum(z + 1, span - 1) * slots + own
+    lower = jnp.maximum(z - 1, 0) * slots + own
+
+    def row_copy(i, device, spare):
         return pltpu.make_async_remote_copy(
-            src_ref=src,
-            dst_ref=dst,
-            send_sem=send_sem.at[i],
-            recv_sem=recv_sem.at[i],
+            src_ref=tok.at[0, 0, i],
+            dst_ref=tok.at[0, 0, i],
+            send_sem=chain_send.at[spare],
+            recv_sem=chain_recv.at[i],
             device_id={"expert": device},
             device_id_type=pl.DeviceIdType.MESH,
         )
 
-    def start(copy):
-        copy.start()
-        sent.append(copy)
-
-    left, right = pl.ds(0, half), pl.ds(half, half + LANES)
-    by_z = {
-        p: message(tok.at[0, 0, 0], tok.at[0, 0, p], along_z(span - p, own)) for p in range(1, span)
-    }
-    by_x = [message(tok.at[0, 0, p], tok.at[1, 0, p], x_peer) for p in range(span)]
-    by_y = [message(tok.at[0, 0, p], tok.at[2, 0, p], y_peer) for p in range(span)]
+    by_x = family(span, lambda i: (tok.at[0, 0, i], tok.at[1, 0, i], x_peer))
+    by_y = family(span, lambda i: (tok.at[0, 0, i], tok.at[2, 0, i], y_peer))
     to_core = [
-        [message(tok.at[g, 0, p], tok.at[g, 1, p], core_peer) for p in range(span)] for g in range(3)
+        family(span, lambda i, g=g: (tok.at[g, 0, i], tok.at[g, 1, i], core_peer)) for g in range(3)
     ]
-    far_left = [
-        message(tok.at[1, 0, p, :, left], tok.at[3, 0, p, :, left], y_peer) for p in range(span)
-    ]
-    far_right = [
-        message(tok.at[2, 0, p, :, right], tok.at[3, 0, p, :, right], x_peer) for p in range(span)
-    ]
-    core_left = [
-        message(tok.at[3, 0, p, :, left], tok.at[3, 1, p, :, left], core_peer) for p in range(span)
-    ]
-    core_right = [
-        message(tok.at[3, 0, p, :, right], tok.at[3, 1, p, :, right], core_peer)
-        for p in range(span)
-    ]
-    swap_down = message(down_hbm.at[0, :, other_half], wd.at[1], core_peer)
-    swap_hidden = [message(hid_out.at[g], hid.at[g, 1], core_peer) for g in range(4)]
-    x_early = message(x_out.at[0], x_in.at[0], x_peer)
-    y_early = message(y_out.at[1], y_in.at[1], y_peer)
-    d_to_x = [message(d_out.at[0, p], d_in.at[0, p], x_peer) for p in range(span)]
-    d_to_y = [message(d_out.at[1, p], d_in.at[1, p], y_peer) for p in range(span)]
-    x_late = [message(x_out.at[1, p], x_in.at[1, p], x_peer) for p in range(span)]
-    y_late = [message(y_out.at[0, p], y_in.at[0, p], y_peer) for p in range(span)]
+    far_left = family(
+        span, lambda i: (tok.at[1, 0, i, :, left], tok.at[3, 0, i, :, left], y_peer)
+    )
+    far_right = family(
+        span, lambda i: (tok.at[2, 0, i, :, right], tok.at[3, 0, i, :, right], x_peer)
+    )
+    core_left = family(
+        span, lambda i: (tok.at[3, 0, i, :, left], tok.at[3, 1, i, :, left], core_peer)
+    )
+    core_right = family(
+        span, lambda i: (tok.at[3, 0, i, :, right], tok.at[3, 1, i, :, right], core_peer)
+    )
+    swap_down = family(1, lambda i: (down_hbm.at[0, :, other_half], wd.at[1], core_peer))(0)
+    hidden_family = family(4, lambda g: (hid_out.at[g], hid.at[g, 1], core_peer))
+    swap_hidden = [hidden_family(g) for g in range(4)]
+    x_early = family(span, lambda i: (x_out.at[0, i], x_in.at[0, i], x_peer))
+    y_early = family(span, lambda i: (y_out.at[1, i], y_in.at[1, i], y_peer))
+    d_to_x = family(span, lambda i: (d_out.at[0, i], d_in.at[0, i], x_peer))
+    d_to_y = family(span, lambda i: (d_out.at[1, i], d_in.at[1, i], y_peer))
+    x_late = family(span, lambda i: (x_out.at[1, i], x_in.at[1, i], x_peer))
+    y_late = family(span, lambda i: (y_out.at[0, i], y_in.at[0, i], y_peer))
+    home_family = family(
+        2 * span,
+        lambda rp: (
+            z_out.at[rp[0], rp[1]],
+            z_in.at[rp[0], (span - rp[1]) % span],
+            along_z(rp[1], own if rp[0] == 0 else flipped(own, CORE)),
+        ),
+    )
     home = {
-        (r, p): message(
-            z_out.at[r, p],
-            z_in.at[r, (span - p) % span],
-            along_z(p, own if r == 0 else flipped(own, CORE)),
-        )
+        (r, p): home_family((r, p), r * span + p)
         for r in range(2)
         for p in range(span)
         if (r, p) != (0, 0)
@@ -199,93 +231,110 @@
 
         lax.fori_loop(0, half // wide, step, 0)
 
-    def gathered(p):
-        if p:
-            by_z[p].wait_recv()
-        start(by_x[p])
-        start(by_y[p])
-        start(to_core[0][p])
-
-    def crossed(p):
-        by_x[p].wait_recv()
-        start(far_left[p])
-        start(to_core[1][p])
-        by_y[p].wait_recv()
-        start(far_right[p])
-        start(to_core[2][p])
-
-    def cornered(p):
-        far_left[p].wait_recv()
-        start(core_left[p])
-        far_right[p].wait_recv()
-        start(core_right[p])
+    low = z < span // 2
+    arrivals = [flipped(z, 1), jnp.where(low, 2, 1), jnp.where(low, 3, 0)]
+    inner = (z > 0) & (z < span - 1)
+
+    def passed_on(j):
+        i = arrivals[j]
+        return row_copy(i, jnp.where(i < z, upper, lower), 2 + j)
+
+    def gathered(i):
+        start(by_x(i))
+        start(by_y(i))
+        start(to_core[0](i))
+
+    def crossed(i):
+        by_x(i).wait_recv()
+        start(far_left(i))
+        start(to_core[1](i))
+        by_y(i).wait_recv()
+        start(far_right(i))
+        start(to_core[2](i))
+
+    def cornered(i):
+        far_left(i).wait_recv()
+        start(core_left(i))
+        far_right(i).wait_recv()
+        start(core_right(i))
 
     loads[0].wait()
     pl.semaphore_wait(barrier, len(partners))
-    for p in range(1, span):
-        start(by_z[p])
-    gathered(0)
+    pl.when(z < span - 1)(lambda: row_copy(z, upper, 0).start())
+    pl.when(z > 0)(lambda: row_copy(z, lower, 1).start())
+    gathered(z)
     start(swap_down)
-    order = [p for p in (1, span - 1) if p < span] + list(range(2, span - 1))
-    done = [0]
-    for p in order:
-        gathered(p)
+    done = [z]
+    for j, i in enumerate(arrivals):
+        row_copy(i, upper, 2 + j).wait_recv()
+        pl.when(inner)(lambda j=j: passed_on(j).start())
+        gathered(i)
         crossed(done[-1])
         if len(done) > 1:
             cornered(done[-2])
-        done.append(p)
+        done.append(i)
     for load in loads[1:3]:
         load.wait()
-    for p in range(span):
-        to_core[0][p].wait_recv()
+    for i in range(span):
+        to_core[0](i).wait_recv()
     project(0)
     crossed(done[-1])
     cornered(done[-2])
-    for p in range(span):
-        to_core[1][p].wait_recv()
+    for i in range(span):
+        to_core[1](i).wait_recv()
     project(1)
     cornered(done[-1])
-    for p in range(span):
-        to_core[2][p].wait_recv()
+    for i in range(span):
+        to_core[2](i).wait_recv()
     project(2)
     loads[3].wait()
     swap_down.wait_recv()
     expand(1, x_out.at[0], x_pend)
-    start(x_early)
     expand(2, y_pend, y_out.at[1])
-    start(y_early)
-    for p in range(span):
-        core_left[p].wait_recv()
-        core_right[p].wait_recv()
+    order = [(p, (z + p) % span) for p in (2, 3, 1, 0)]
+    ahead = 2
+    for _, i in order[:ahead]:
+        start(x_early(i))
+        start(y_early(i))
+    for i in range(span):
+        core_left(i).wait_recv()
+        core_right(i).wait_recv()
     project(3)
     expand(0, own_sum.at[0], own_sum.at[1])
     expand(3, d_out.at[0], d_out.at[1])
-    order = order + [0]
-    for p in order:
-        start(d_to_x[p])
-        start(d_to_y[p])
-    for p in order:
-        d_to_y[p].wait_recv()
-        x_out[1, p] = (x_pend[p] + d_in[1, p].astype(jnp.float32)).astype(jnp.bfloat16)
-        start(x_late[p])
-        d_to_x[p].wait_recv()
-        y_out[0, p] = (y_pend[p] + d_in[0, p].astype(jnp.float32)).astype(jnp.bfloat16)
-        start(y_late[p])
-    x_early.wait_recv()
-    y_early.wait_recv()
-    for p in order:
-        x_late[p].wait_recv()
-        y_late[p].wait_recv()
+    for _, i in order[:ahead]:
+        start(d_to_x(i))
+        start(d_to_y(i))
+
+    def finish(p, i):
+        for copy in (x_early(i), y_early(i), x_late(i), y_late(i)):
+            copy.wait_recv()
         for r in range(2):
-            total = own_sum[r, p] + x_in[r, p].astype(jnp.float32) + y_in[r, p].astype(jnp.float32)
+            total = own_sum[r, i] + x_in[r, i].astype(jnp.float32) + y_in[r, i].astype(jnp.float32)
             if (r, p) == (0, 0):
-                own_sum[r, p] = total
+                own_sum[r, i] = total
             else:
                 z_out[r, p] = total.astype(jnp.bfloat16)
                 start(home[r, p])
+
+    for n, (p, i) in enumerate(order):
+        d_to_y(i).wait_recv()
+        x_out[1, i] = (x_pend[i] + d_in[1, i].astype(jnp.float32)).astype(jnp.bfloat16)
+        start(x_late(i))
+        d_to_x(i).wait_recv()
+        y_out[0, i] = (y_pend[i] + d_in[0, i].astype(jnp.float32)).astype(jnp.bfloat16)
+        start(y_late(i))
+        if n + ahead < span:
+            start(x_early(order[n + ahead][1]))
+            start(y_early(order[n + ahead][1]))
+            start(d_to_x(order[n + ahead][1]))
+            start(d_to_y(order[n + ahead][1]))
+        if n:
+            finish(*order[n - 1])
+    finish(*order[-1])
     for copy in home.values():
         copy.wait_recv()
-    total = own_sum[0, 0]
+    total = own_sum[0, z]
     for p in range(1, span):
         total += z_in[0, p].astype(jnp.float32)
     out_ref[:, my_half] = total.astype(jnp.bfloat16)
@@ -295,6 +344,10 @@
     out_ref[:, other_half] = total.astype(jnp.bfloat16)
     for copy in sent:
         copy.wait_send()
+    pl.when(z < span - 1)(lambda: row_copy(z, upper, 0).wait_send())
+    pl.when(z > 0)(lambda: row_copy(z, lower, 1).wait_send())
+    for j in range(span - 1):
+        pl.when(inner)(lambda j=j: passed_on(j).wait_send())
 
 
 def squares(tokens, slot_ids, route_weights, pair_swap, w_gate, w_up, w_down):
@@ -304,7 +357,7 @@
     half = width // 2
     wide = width + LANES
     group = 2 * span * rows
-    messages = (span - 1) + 9 * span + 1 + 4 + 2 + 4 * span + 2 * span - 1
+    messages = 9 * span + 1 + 4 + 6 * span + 2 * span + 4 + span
     bf16, f32 = jnp.bfloat16, jnp.float32
     column = (span, rows, half)
     vmem = pl.BlockSpec(memory_space=pltpu.VMEM)
@@ -332,11 +385,13 @@
             pltpu.SemaphoreType.DMA((4,)),
             pltpu.SemaphoreType.DMA((messages,)),
             pltpu.SemaphoreType.DMA((messages,)),
+            pltpu.SemaphoreType.DMA((span + 1,)),
+            pltpu.SemaphoreType.DMA((span,)),
         ],
         compiler_params=pltpu.CompilerParams(
             collective_id=0, has_side_effects=True, vmem_limit_bytes=56 * 2**20
         ),
-    )(pair_swap, slot_ids, route_weights, tokens, w_gate, w_up, w_down)
+    )(pair_swap, slot_ids.T, route_weights.T, tokens, w_gate, w_up, w_down)
 
 
 def whole(tokens, slot_ids, route_weights, pair_swap, w_gate, w_up, w_down):
@@ -361,7 +416,8 @@
 
 def on_device(*args):
     slots = 2 * args[3].shape[0]
-    return (squares if slots == SQUARE_SLOTS else whole)(*args)
+    square = slots == SQUARE_SLOTS and lax.axis_size("expert") == SQUARE_SLOTS * COLUMN
+    return (squares if square else whole)(*args)
 
 
 def solution(mesh):

time: 102 us -> 85.9 us (0.84)
  Pallas kernels: 97.2 us -> 84.1 us
  local copies, waits for them, and re-layouts: 4.35 us -> 1.64 us
    pallas_call x1, Pallas kernels: 97.2 us -> 84.1 us  [squares(): pl.pallas_call(functools.partial(kernel, span), out_shape=jax.ShapeDtypeS...]
    unnamed x3 -> x1, local copies, waits for them, and re-layouts: 4.35 us -> 1.64 us
where the time goes in v2:
time: 85.9 us; the launch traced here: 85.7 us
  Pallas kernels  84.1 us (98%)
  local copies, waits for them, and re-layouts  1.64 us (2%)
    pallas_call x1, Pallas kernels, squares(): pl.pallas_call(functools.partial(kernel, span), out_shape=jax.ShapeDtypeS...  84.1 us

profile of v2, /device:TPU:1, one launch (start us, length us, event | category | flops | bytes accessed | tf_op | source)
XLA Modules:
  0.0 85.7 jit_solution(13771576806167939148)
XLA Ops:
  0.0 84.1 %shard_map.73 = bf16[16,7168]{1,0:T(8,128)(2,1)} custom-call(s32[4]{0:T(128)} %pair_ref.1, s32[4,16]{1,0:T(4,128)} %bitcast.2, f32[4,16]{1,0:T(4,128)} %bitcast.3, bf16[16,7168]{1,0:T(8,128)(2,1)} %tokens_hbm.1, bf16[1,7168,256]{2,1,0:T(8,128)(2,1)} %gate_hbm.1, bf16[1,7168,256]{2,1,0:T(8,128)(2,1)} %up_hbm.1, bf16[1,256,7168]{2,1,0:T(8,128)(2,1)} %down_hbm.1), custom_call_target="tpu_custom_call" | custom-call | tf_op jit(solution)/shard_map/pallas_call | solution.py:365
  84.1 1.6 %copy.9 = bf16[16,7168]{1,0:T(8,128)(2,1)} copy(bf16[16,7168]{1,0:T(8,128)(2,1)} %shard_map.73) | data formatting | bytes 458752

commit v3 on v2

--- a/solution.py
+++ b/solution.py
@@ -191,7 +191,7 @@
     }
 
     def project(g):
-        depth = 1024 if width % 1024 == 0 else width
+        depth = 1792 if width % 1792 == 0 else width
         gate_acc[...] = jnp.zeros_like(gate_acc)
         up_acc[...] = jnp.zeros_like(up_acc)
 
@@ -217,7 +217,7 @@
         start(swap_hidden[g])
 
     def expand(g, first_to, second_to):
-        wide = 512 if half % 512 == 0 else half
+        wide = 1792 if half % 1792 == 0 else half
         many = span * rows
         swap_hidden[g].wait_recv()
 

time: 85.9 us -> 83.9 us (0.977)
  Pallas kernels: 84.1 us -> 82.1 us
    pallas_call x1, Pallas kernels: 84.1 us -> 82.1 us  [squares(): pl.pallas_call(functools.partial(kernel, span), out_shape=jax.ShapeDtypeS...]
where the time goes in v3:
time: 83.9 us; the launch traced here: 83.8 us
  Pallas kernels  82.1 us (98%)
  local copies, waits for them, and re-layouts  1.64 us (2%)
    pallas_call x1, Pallas kernels, squares(): pl.pallas_call(functools.partial(kernel, span), out_shape=jax.ShapeDtypeS...  82.1 us

profile of v3, /device:TPU:1, one launch (start us, length us, event | category | flops | bytes accessed | tf_op | source)
XLA Modules:
  0.0 83.8 jit_solution(16336651818405119451)
XLA Ops:
  0.0 82.1 %shard_map.73 = bf16[16,7168]{1,0:T(8,128)(2,1)} custom-call(s32[4]{0:T(128)} %pair_ref.1, s32[4,16]{1,0:T(4,128)} %bitcast.2, f32[4,16]{1,0:T(4,128)} %bitcast.3, bf16[16,7168]{1,0:T(8,128)(2,1)} %tokens_hbm.1, bf16[1,7168,256]{2,1,0:T(8,128)(2,1)} %gate_hbm.1, bf16[1,7168,256]{2,1,0:T(8,128)(2,1)} %up_hbm.1, bf16[1,256,7168]{2,1,0:T(8,128)(2,1)} %down_hbm.1), custom_call_target="tpu_custom_call" | custom-call | tf_op jit(solution)/shard_map/pallas_call | solution.py:365
  82.1 1.6 %copy.9 = bf16[16,7168]{1,0:T(8,128)(2,1)} copy(bf16[16,7168]{1,0:T(8,128)(2,1)} %shard_map.73) | data formatting | bytes 458752
